TPU v7x, 128 devices: a whole 4x4x4 slice. The times are simulated.
128 devices in a mesh: tok: 32 (over y, x_lo, z), rep: 4 (over x_hi, core).
Axes of the slice: x: 4 (x_hi: 2, x_lo: 2; x = x_hi * 2 + x_lo), y: 4, z: 4, core: 2. Of those that a mesh axis runs over, the one named last changes fastest.
Arguments:
- tokens: bfloat16 [65536, 768], P(('rep', 'tok')), parts along dimension 0, may hold values from -6 to 6
- attn_gain: bfloat16 [768], replicated, may hold values from 0.25 to 1.75
- qkv_weight: bfloat16 [768, 2304], replicated, may hold values from -0.21875 to 0.21875
- head_temp: float32 [12], replicated, may hold values from 2 to 600, as said below
- out_weight: bfloat16 [768, 768], replicated, may hold values from -0.21875 to 0.21875
- kv_weight: bfloat16 [768, 1536], replicated, may hold values from -0.21875 to 0.21875
- rate_weight: float32 [768, 2], replicated, may hold values from -0.21875 to 0.21875
- fast_weights: bfloat16 [768, 2304], replicated, may hold values from -0.3125 to 0.3125
- target: bfloat16 [32768, 768], P(('rep', 'tok')), parts along dimension 0, may hold values from -6 to 6
- query_weight: bfloat16 [768, 768], replicated, may hold values from -0.21875 to 0.21875
- merge_weight: bfloat16 [768, 768], replicated, may hold values from -0.21875 to 0.21875
- image_lengths: int32 [64], P('rep'), parts along dimension 0, may hold values from 512 to 1024, as said below
- target_counts: int32 [128], P(('rep', 'tok')), parts along dimension 0, may hold values from 64 to 256, as said below
Outputs:
- tokens_out: bfloat16 [65536, 768], P(('rep', 'tok')), parts along dimension 0
- fast_updated: bfloat16 [3072, 2304], P(('rep', 'tok')), parts along dimension 0
- target_out: bfloat16 [32768, 768], P(('rep', 'tok')), parts along dimension 0
There are 4 independent parts, one for each index of `rep`. A program takes and returns all parts, laid end to end along the dimension named above; an argument that names none is the same for every part. Nothing has to cross between parts.
Inputs may be any that keep to these rules, and one draw needn't show every extreme that they name: `image_lengths`: every image has at least half of its 1024 slots valid, and some image of every scene is full. `target_counts`: some device of every scene uses all 256 slots. `head_temp`: positive score scales.
All inputs are finite; a program needn't handle non-finite values.
Results may differ from a plain program's by a relative error of at most 0.025.
The roundings to bfloat16 on the way count: a program that leaves them out, or rounds other values in their place, can miss the bound.
Values may be sent and summed in bfloat16 or wider, within the bound.
No kernel may reach another device: no remote copies, remote signals or barrier semaphores. Data moves between devices by JAX's collectives and lax.ppermute only.
A program may use at most 192 MiB of HBM per device.

v0:
```python
import jax
import jax.numpy as jnp
from jax import lax
from jax.sharding import PartitionSpec as P

eps = 1e-06
rate_base = 4.0


def partner(value, axis, bit):
    mask = 2**bit
    pairs = [(source, source ^ mask) for source in range(lax.axis_size(axis))]
    return lax.ppermute(value, axis, pairs)


def unit_rows(values):
    values = values.astype(jnp.float32)
    return values * lax.rsqrt(jnp.mean(values * values, axis=-1, keepdims=True) + eps)


def attend(query, keyset, valueset, temps, valid):
    head_dim = query.shape[-1]
    qhat = unit_rows(query).astype(jnp.bfloat16)
    khat = unit_rows(keyset).astype(jnp.bfloat16)
    scores = jnp.einsum("qhd,khd->hqk", qhat, khat, preferred_element_type=jnp.float32)
    scores = scores * (temps / head_dim)[:, None, None]
    scores = jnp.where(valid[None, None, :], scores, -1e30)
    top = jnp.max(scores, axis=-1, keepdims=True)
    expo = jnp.exp(scores - top)
    weights = (expo / jnp.sum(expo, axis=-1, keepdims=True)).astype(jnp.bfloat16)
    result = jnp.einsum("hqk,khd->qhd", weights, valueset, preferred_element_type=jnp.float32)
    return result.astype(jnp.bfloat16)


def rescale(start_rows, grad, fast_heads, fast_dim):
    count = start_rows.shape[0]
    start_w = start_rows.astype(jnp.float32).reshape(count, 3 * fast_heads, fast_dim)
    update = start_w - grad.reshape(count, 3 * fast_heads, fast_dim)
    fresh = (
        update
        * jnp.sqrt(jnp.mean(start_w * start_w, axis=-1, keepdims=True) + eps)
        * lax.rsqrt(jnp.mean(update * update, axis=-1, keepdims=True) + eps)
    )
    return fresh.reshape(count, 3 * fast_heads * fast_dim).astype(jnp.bfloat16)


def body(
    tokens,
    attn_gain,
    qkv_weight,
    head_temp,
    out_weight,
    kv_weight,
    rate_weight,
    fast_weights,
    target,
    query_weight,
    merge_weight,
    image_lengths,
    target_counts,
):
    tok_rows, width = tokens.shape
    devices = lax.axis_size("tok")
    place = lax.axis_index("tok")
    parity = place % 2
    heads = head_temp.shape[0]
    head_dim = width // heads
    half = heads // 2
    fast_hidden = fast_weights.shape[0]
    fast_heads = rate_weight.shape[1]
    fast_dim = width // fast_heads
    image_ids = jnp.arange(image_lengths.shape[0], dtype=jnp.int32)
    my_length = jnp.sum(jnp.where(image_ids == place // 2, image_lengths, 0))
    inputs = tokens.astype(jnp.float32)
    normed = (unit_rows(inputs) * attn_gain.astype(jnp.float32)).astype(jnp.bfloat16)
    qkv = jnp.dot(normed, qkv_weight, preferred_element_type=jnp.float32).astype(jnp.bfloat16)
    qkv = qkv.reshape(tok_rows, 3, heads, head_dim)
    key_valid = jnp.arange(2 * tok_rows, dtype=jnp.int32) < my_length
    leading = parity == 0
    owned = lax.dynamic_slice_in_dim(qkv, parity * half, half, 2)
    other = lax.dynamic_slice_in_dim(qkv, (1 - parity) * half, half, 2)
    arrived = partner(other.reshape(tok_rows, 3 * half * head_dim), "tok", 0)
    arrived = arrived.reshape(tok_rows, 3, half, head_dim)
    joined = jnp.concatenate(
        [jnp.where(leading, owned, arrived), jnp.where(leading, arrived, owned)], axis=0
    )
    temps = lax.dynamic_slice_in_dim(head_temp, parity * half, half, 0)
    result = attend(joined[:, 0], joined[:, 1], joined[:, 2], temps, key_valid)
    mine = jnp.where(leading, result[:tok_rows], result[tok_rows:])
    theirs = jnp.where(leading, result[tok_rows:], result[:tok_rows])
    returned = partner(theirs.reshape(tok_rows, half * head_dim), "tok", 0)
    returned = returned.reshape(tok_rows, half, head_dim)
    lower = jnp.where(leading, mine, returned)
    upper = jnp.where(leading, returned, mine)
    attn = jnp.concatenate([lower, upper], axis=1).reshape(tok_rows, width)
    tokens_out = (inputs + jnp.dot(attn, out_weight, preferred_element_type=jnp.float32)).astype(
        jnp.bfloat16
    )
    kv = jnp.dot(tokens_out, kv_weight, preferred_element_type=jnp.float32)
    own_valid = parity * tok_rows + jnp.arange(tok_rows, dtype=jnp.int32) < my_length
    logit = jnp.dot(tokens_out.astype(jnp.float32), rate_weight, precision=lax.Precision.HIGHEST)
    rate = (
        jax.nn.softplus(logit + 1.0)
        * (rate_base / (tok_rows * devices))
        * own_valid[:, None].astype(jnp.float32)
    )
    pieces = []
    for head in range(fast_heads):
        keys = unit_rows(kv[:, head * fast_dim : (head + 1) * fast_dim]).astype(jnp.bfloat16)
        values = kv[:, width + head * fast_dim : width + (head + 1) * fast_dim]
        base = 3 * head * fast_dim
        act_a = jnp.dot(
            keys, fast_weights[:, base : base + fast_dim].T, preferred_element_type=jnp.float32
        )
        act_b = jnp.dot(
            keys,
            fast_weights[:, base + fast_dim : base + 2 * fast_dim].T,
            preferred_element_type=jnp.float32,
        )
        hidden = (jax.nn.silu(act_a) * act_b).astype(jnp.bfloat16)
        push = (-rate[:, head : head + 1] * values).astype(jnp.bfloat16)
        back_h = jnp.dot(
            push,
            fast_weights[:, base + 2 * fast_dim : base + 3 * fast_dim].T,
            preferred_element_type=jnp.float32,
        )
        sigma = jax.nn.sigmoid(act_a)
        grad_a = (back_h * act_b * sigma * (1.0 + act_a * (1.0 - sigma))).astype(jnp.bfloat16)
        grad_b = (back_h * jax.nn.silu(act_a)).astype(jnp.bfloat16)
        pieces.append((keys, push, hidden, grad_a, grad_b))
    tq = jnp.dot(target, query_weight, preferred_element_type=jnp.float32)
    queries = [
        unit_rows(tq[:, head * fast_dim : (head + 1) * fast_dim]).astype(jnp.bfloat16)
        for head in range(fast_heads)
    ]
    rows = fast_hidden // devices
    blocks = []
    for keys, push, hidden, grad_a, grad_b in pieces:
        blocks.append(jnp.dot(grad_a.T, keys, preferred_element_type=jnp.float32))
        blocks.append(jnp.dot(grad_b.T, keys, preferred_element_type=jnp.float32))
        blocks.append(jnp.dot(hidden.T, push, preferred_element_type=jnp.float32))
    grad_mine = lax.psum_scatter(
        jnp.concatenate(blocks, axis=1).astype(jnp.bfloat16), "tok", scatter_dimension=0, tiled=True
    ).astype(jnp.float32)
    start_rows = lax.dynamic_slice_in_dim(fast_weights, place * rows, rows, 0)
    fresh = rescale(start_rows, grad_mine, fast_heads, fast_dim)
    piece = lax.all_gather(fresh, "tok", axis=0, tiled=True)
    results = []
    for apply_head in range(fast_heads):
        base = 3 * apply_head * fast_dim
        act_a = jnp.dot(
            queries[apply_head],
            piece[:, base : base + fast_dim].T,
            preferred_element_type=jnp.float32,
        )
        act_b = jnp.dot(
            queries[apply_head],
            piece[:, base + fast_dim : base + 2 * fast_dim].T,
            preferred_element_type=jnp.float32,
        )
        hidden_t = (jax.nn.silu(act_a) * act_b).astype(jnp.bfloat16)
        results.append(
            jnp.dot(
                hidden_t,
                piece[:, base + 2 * fast_dim : base + 3 * fast_dim],
                preferred_element_type=jnp.float32,
            )
        )
    outputs = jnp.stack(results, axis=0)
    fout = jnp.concatenate(
        [unit_rows(outputs[head]).astype(jnp.bfloat16) for head in range(fast_heads)], axis=1
    )
    merged = target.astype(jnp.float32) + jnp.dot(
        fout, merge_weight, preferred_element_type=jnp.float32
    )
    used = jnp.arange(target.shape[0], dtype=jnp.int32) < target_counts[0]
    target_out = jnp.where(used[:, None], merged, 0.0).astype(jnp.bfloat16)
    return (tokens_out, fresh, target_out)


def solution(mesh):
    placed = (
        P(("rep", "tok"), None),
        P(),
        P(),
        P(),
        P(),
        P(),
        P(),
        P(),
        P(("rep", "tok"), None),
        P(),
        P(),
        P("rep"),
        P(("rep", "tok")),
    )
    return jax.shard_map(
        body,
        mesh=mesh,
        in_specs=placed,
        out_specs=(P(("rep", "tok"), None), P(("rep", "tok"), None), P(("rep", "tok"), None)),
        check_vma=False,
    )
```

profile of v0, /device:TPU:0, one launch (start us, length us, event | category | flops | bytes accessed | tf_op | source)
XLA Modules:
  0.0 453.7 jit_solution(13452142345628719340)
XLA Ops:
  7.2 1.5 fusion.12
  9.5 4.6 %convolution_convert_fusion = bf16[512,2304]{1,0:T(8,128)(2,1)} fusion(bf16[768,2304]{1,0:T(8,128)(2,1)S(1)} %copy-done, bf16[512,768]{1,0:T(8,128)(2,1)} %param.13, f32[768]{0:T(1024)S(1)} %convert_element_type.114, f32[512]{0:T(512)S(1)} %add_rsqrt_fusion.5), kind=kOutput, calls=%fused_computation.9 | convolution fusion | flops 1814691840 | bytes 6689792 | tf_op jit(solution)/shard_map/dot_general | solution.py:76
  14.1 2.8 copy.24
  17.0 1.1 constant_dynamic-slice_fusion.1
  18.1 2.0 collective-permute-start
  21.5 24.8 %collective-permute-done = bf16[512,1152]{0,1:T(8,128)(2,1)S(1)} collective-permute-done((bf16[512,1152]{0,1:T(8,128)(2,1)}, bf16[512,1152]{0,1:T(8,128)(2,1)S(1)}, u32[]{:S(2)}, u32[]{:S(2)}) %collective-permute-start) | collective-permute-done | bytes 1179680 | tf_op jit(solution)/shard_map/ppermute | solution.py:13
  46.3 1.0 copy-done.5
  47.3 1.4 broadcast_select_fusion.1
  48.7 1.3 fusion.8
  50.1 14.4 %fusion.117 = (f32[6,1024]{1,0:T(8,128)S(1)}, f32[6,1024,1024]{1,2,0:T(8,128)}) fusion(f32[6]{0:T(128)S(1)} %dynamic-slice_multiply_fusion, pred[1024]{0:T(1024)(128)(4,1)S(1)} %iota_compare_fusion, bf16[1024,6,64]{0,2,1:T(8,128)(2,1)} %get-tuple-element.25, f32[1024,6]{0,1:T(8,128)S(1)} %get-tuple-element.38, ...), kind=kOutput, calls=%fused_computation.172 | convolution fusion | flops 832832512 | bytes 26813464 | tf_op jit(solution)/shard_map/sub | solution.py:29
  64.5 9.4 %fusion.26 = bf16[1024,6,64]{0,2,1:T(8,128)(2,1)S(1)} fusion(f32[6,1024,1024]{1,2,0:T(8,128)} %get-tuple-element.33, f32[6,1024]{1,0:T(8,128)S(1)} %get-tuple-element.32, bf16[512,3,6,64]{0,3,2,1:T(8,128)(2,1)S(1)} %get-tuple-element.20, bf16[512,3,6,64]{0,3,2,1:T(8,128)(2,1)S(1)} %copy-done.3), kind=kOutput, calls=%fused_computation.59 | convolution fusion | flops 819855360 | bytes 28336128 | tf_op jit(solution)/shard_map/hqk,khd->qhd/dot_general | solution.py:31
  74.0 2.0 collective-permute-start.1
  76.7 7.9 %collective-permute-done.1 = bf16[512,384]{0,1:T(8,128)(2,1)S(1)} collective-permute-done((bf16[512,384]{0,1:T(8,128)(2,1)S(1)}, bf16[512,384]{0,1:T(8,128)(2,1)S(1)}, u32[]{:S(2)}, u32[]{:S(2)}) %collective-permute-start.1) | collective-permute-done | bytes 393248 | tf_op jit(solution)/shard_map/ppermute | solution.py:13
  87.7 1.4 fusion.130
  89.6 1.5 copy-done.4
  95.6 1.8 fusion.24
  97.3 1.6 fusion.23
  98.9 1.6 fusion.22
  100.5 1.8 fusion.21
  102.3 1.6 fusion.20
  103.9 1.6 fusion.19
  105.5 5.8 %copy.30 = bf16[768,2304]{1,0:T(8,128)(2,1)} copy(bf16[768,2304]{0,1:T(8,128)(2,1)} %fusion.19) | data formatting | bytes 7077888
  112.3 1.2 copy.32
  113.5 166.8 %reduce-scatter.4.cloned.1.call-done = bf16[24,2304]{1,0:T(8,128)(2,1)} async-done(((bf16[768,2304]{1,0:T(8,128)(2,1)}), bf16[24,2304]{1,0:T(8,128)(2,1)}) %reduce-scatter.4.cloned.1.call-update) | async-done | bytes 110608
  280.3 1.2 copy.31
  284.5 150.8 %all-gather.2.cloned.1.call-done = bf16[768,2304]{1,0:T(8,128)(2,1)} async-done(((bf16[24,2304]{1,0:T(8,128)(2,1)}), bf16[768,2304]{1,0:T(8,128)(2,1)}) %all-gather.2.cloned.1.call-update) | async-done | bytes 3538960 | tf_op jit(solution)/shard_map/all_gather | solution.py:147
  435.2 1.5 fusion.74
  436.7 2.0 multiply_reduce_fusion.4
  438.7 1.5 fusion.69
  440.2 2.7 multiply_reduce_fusion.2
  443.0 1.2 multiply_convert_fusion.14
  444.3 2.6 fusion.27
  (70 shorter events, 14.1 us)
Async XLA Ops:
  7.2 2.3 copy-start
  7.2 273.2 %reduce-scatter.4.cloned.1.call-start = ((), (), s32[]{:S(2)}) async-start(), calls=%async_computation.2 | async-start | bytes 3649536
  16.9 3.1 copy-start.13
  16.9 3.2 copy-start.14
  18.1 28.2 %collective-permute-start = (bf16[512,1152]{0,1:T(8,128)(2,1)}, bf16[512,1152]{0,1:T(8,128)(2,1)S(1)}, u32[]{:S(2)}, u32[]{:S(2)}) collective-permute-start(bf16[512,1152]{0,1:T(8,128)(2,1)} %bitcast.1), channel_id=1, source_target_pairs={{0,4},{4,0},{8,12},{12,8},{16,20},{20,16},{24,28},{28,24},{32,36},... | collective-permute-start | bytes 3538952 | tf_op jit(solution)/shard_map/ppermute | solution.py:13
  46.3 1.0 copy-start.5
  48.7 1.3 copy-start.2
  50.0 14.4 %copy-start.3 = (bf16[512,3,6,64]{0,3,2,1:T(8,128)(2,1)S(1)}, bf16[512,3,6,64]{0,3,2,1:T(8,128)(2,1)}, u32[]{:S(2)}) copy-start(bf16[512,3,6,64]{0,3,2,1:T(8,128)(2,1)} %copy-done.2) | copy-start | bytes 3538948
  74.0 10.5 %collective-permute-start.1 = (bf16[512,384]{0,1:T(8,128)(2,1)S(1)}, bf16[512,384]{0,1:T(8,128)(2,1)S(1)}, u32[]{:S(2)}, u32[]{:S(2)}) collective-permute-start(bf16[512,384]{0,1:T(8,128)(2,1)S(1)} %bitcast.59), channel_id=1, source_target_pairs={{0,4},{4,0},{8,12},{12,8},{16,20},{20,16},{24,28},{28,24},{32,36},... | collective-permute-start | bytes 1179656 | tf_op jit(solution)/shard_map/ppermute | solution.py:13
  84.5 1.1 copy-start.7
  84.5 1.5 copy-start.12
  86.0 1.7 copy-start.11
  87.7 5.8 %copy-start.8 = (bf16[512,768]{1,0:T(8,128)(2,1)}, bf16[512,768]{1,0:T(8,128)(2,1)S(1)}, u32[]{:S(2)}) copy-start(bf16[512,768]{1,0:T(8,128)(2,1)S(1)} %fusion.15) | copy-start | bytes 2359300
  89.1 2.0 copy-start.4
  92.9 0.7 copy-start.10
  111.3 323.9 %all-gather.2.cloned.1.call-start = ((), (), s32[]{:S(2)}) async-start(), calls=%async_computation.1 | async-start | bytes 3649536 | tf_op jit(solution)/shard_map/all_gather | solution.py:147
  282.0 1.8 copy-start.6
  282.0 1.8 copy-start.9
  443.0 3.9 copy-start.1
Sparse Core Ops, SparseCore 0:
  111.5 168.8 reduce-scatter.3
  283.3 151.9 all-gather.1
where the time goes:
time: 454 us
  waiting for transfers between devices  350 us (77%)
  matrix products  55.7 us (12%)
  local copies, waits for them, and re-layouts  18.6 us (4%)
  between operations  15.1 us (3%)
  other arithmetic  9.74 us (2%)
    unnamed x3, waiting for transfers between devices  167 us
    all_gather x1, waiting for transfers between devices, body(): piece = lax.all_gather(fresh, 'tok', axis=0, tiled=True)  151 us
    ppermute x2, waiting for transfers between devices, partner(): return lax.ppermute(value, axis, pairs)  32.7 us
    sub x1, matrix products, attend(): expo = jnp.exp(scores - top)  14.4 us
    unnamed x34, local copies, waits for them, and re-layouts  14 us
    dot_general x1, matrix products, attend(): jnp.einsum('hqk,khd->qhd', weights, valueset, preferred_element_type=jnp....  9.44 us
  transfers between devices with their start and end apart: 4, of which 4 were waited for; matrix products, arithmetic and copies ran while one was open for 1% of the time, Pallas kernels for 0%

commit v1 on v0

--- a/solution.py
+++ b/solution.py
@@ -144,7 +144,9 @@
     ).astype(jnp.float32)
     start_rows = lax.dynamic_slice_in_dim(fast_weights, place * rows, rows, 0)
     fresh = rescale(start_rows, grad_mine, fast_heads, fast_dim)
-    piece = lax.all_gather(fresh, "tok", axis=0, tiled=True)
+    piece = jnp.concatenate(
+        lax.all_to_all(jnp.stack([fresh] * lax.axis_size("tok")), "tok", 0, 0), axis=0
+    )
     results = []
     for apply_head in range(fast_heads):
         base = 3 * apply_head * fast_dim

time: 454 us -> 348 us (0.77)
  waiting for transfers between devices: 350 us -> 237 us
  starting transfers between devices: 4.31 us -> 9.22 us
    all_gather x1 -> x0, waiting for transfers between devices: 151 us -> none  [body(): piece = lax.all_gather(fresh, 'tok', axis=0, tiled=True)]
    all_to_all x0 -> x1, waiting for transfers between devices: none -> 28.9 us  [body(): lax.all_to_all(jnp.stack([fresh] * lax.axis_size('tok')), 'tok', 0, 0)]
    unnamed x3 -> x2, waiting for transfers between devices: 167 us -> 176 us
    all_to_all x0 -> x1, starting transfers between devices: none -> 5.18 us  [body(): lax.all_to_all(jnp.stack([fresh] * lax.axis_size('tok')), 'tok', 0, 0)]
    unnamed x34 -> x36, local copies, waits for them, and re-layouts: 14 us -> 13.4 us
where the time goes in v1:
time: 348 us; the launch traced here: 347 us
  waiting for transfers between devices  237 us (68%)
  matrix products  55.7 us (16%)
  local copies, waits for them, and re-layouts  20 us (6%)
  between operations  15.1 us (4%)
  other arithmetic  9.74 us (3%)
  starting transfers between devices  9.22 us (3%)
    unnamed x2, waiting for transfers between devices  176 us
    ppermute x2, waiting for transfers between devices, partner(): return lax.ppermute(value, axis, pairs)  32.7 us
    all_to_all x1, waiting for transfers between devices, body(): lax.all_to_all(jnp.stack([fresh] * lax.axis_size('tok')), 'tok', 0, 0)  28.9 us
    sub x1, matrix products, attend(): expo = jnp.exp(scores - top)  14.4 us
    unnamed x36, local copies, waits for them, and re-layouts  13.4 us
    dot_general x1, matrix products, attend(): jnp.einsum('hqk,khd->qhd', weights, valueset, preferred_element_type=jnp....  9.44 us
  transfers between devices with their start and end apart: 4, of which 4 were waited for; matrix products, arithmetic and copies ran while one was open for 1% of the time, Pallas kernels for 0%

profile of v1, /device:TPU:0, one launch (start us, length us, event | category | flops | bytes accessed | tf_op | source)
XLA Modules:
  0.0 347.0 jit_solution(17155009021787018312)
XLA Ops:
  7.2 1.5 fusion.12
  9.5 4.6 %convolution_convert_fusion = bf16[512,2304]{1,0:T(8,128)(2,1)} fusion(bf16[768,2304]{1,0:T(8,128)(2,1)S(1)} %copy-done, bf16[512,768]{1,0:T(8,128)(2,1)} %param.13, f32[768]{0:T(1024)S(1)} %convert_element_type.114, f32[512]{0:T(512)S(1)} %add_rsqrt_fusion.5), kind=kOutput, calls=%fused_computation.9 | convolution fusion | flops 1814691840 | bytes 6689792 | tf_op jit(solution)/shard_map/dot_general | solution.py:76
  14.1 2.8 copy.26
  18.1 2.0 collective-permute-start
  21.5 24.8 %collective-permute-done = bf16[512,1152]{0,1:T(8,128)(2,1)S(1)} collective-permute-done((bf16[512,1152]{0,1:T(8,128)(2,1)}, bf16[512,1152]{0,1:T(8,128)(2,1)S(1)}, u32[]{:S(2)}, u32[]{:S(2)}) %collective-permute-start) | collective-permute-done | bytes 1179680 | tf_op jit(solution)/shard_map/ppermute | solution.py:13
  47.3 1.4 broadcast_select_fusion.1
  48.7 1.3 fusion.8
  50.1 14.4 %fusion.117 = (f32[6,1024]{1,0:T(8,128)S(1)}, f32[6,1024,1024]{1,2,0:T(8,128)}) fusion(f32[6]{0:T(128)S(1)} %dynamic-slice_multiply_fusion, pred[1024]{0:T(1024)(128)(4,1)S(1)} %iota_compare_fusion, bf16[1024,6,64]{0,2,1:T(8,128)(2,1)} %get-tuple-element.25, f32[1024,6]{0,1:T(8,128)S(1)} %get-tuple-element.38, ...), kind=kOutput, calls=%fused_computation.172 | convolution fusion | flops 832832512 | bytes 26813464 | tf_op jit(solution)/shard_map/sub | solution.py:29
  64.5 9.4 %fusion.26 = bf16[1024,6,64]{0,2,1:T(8,128)(2,1)S(1)} fusion(f32[6,1024,1024]{1,2,0:T(8,128)} %get-tuple-element.33, f32[6,1024]{1,0:T(8,128)S(1)} %get-tuple-element.32, bf16[512,3,6,64]{0,3,2,1:T(8,128)(2,1)S(1)} %get-tuple-element.20, bf16[512,3,6,64]{0,3,2,1:T(8,128)(2,1)S(1)} %copy-done.3), kind=kOutput, calls=%fused_computation.59 | convolution fusion | flops 819855360 | bytes 28336128 | tf_op jit(solution)/shard_map/hqk,khd->qhd/dot_general | solution.py:31
  74.0 2.0 collective-permute-start.1
  76.7 7.9 %collective-permute-done.1 = bf16[512,384]{0,1:T(8,128)(2,1)S(1)} collective-permute-done((bf16[512,384]{0,1:T(8,128)(2,1)S(1)}, bf16[512,384]{0,1:T(8,128)(2,1)S(1)}, u32[]{:S(2)}, u32[]{:S(2)}) %collective-permute-start.1) | collective-permute-done | bytes 393248 | tf_op jit(solution)/shard_map/ppermute | solution.py:13
  87.7 1.4 fusion.130
  89.6 1.5 copy-done.4
  95.6 1.8 fusion.24
  97.3 1.6 fusion.23
  98.9 1.6 fusion.22
  100.5 1.8 fusion.21
  102.3 1.6 fusion.20
  103.9 1.6 fusion.19
  105.5 5.8 %copy.32 = bf16[768,2304]{1,0:T(8,128)(2,1)} copy(bf16[768,2304]{0,1:T(8,128)(2,1)} %fusion.19) | data formatting | bytes 7077888
  112.0 1.2 copy.34
  113.3 175.7 %reduce-scatter.4.cloned.1.call-done = bf16[24,2304]{1,0:T(8,128)(2,1)} async-done(((bf16[768,2304]{1,0:T(8,128)(2,1)}), bf16[24,2304]{1,0:T(8,128)(2,1)}) %reduce-scatter.4.cloned.1.call-update) | async-done | bytes 110608
  288.9 1.2 copy.33
  291.1 2.0 stack.2
  293.1 5.2 %all-to-all-start = ((bf16[32,24,2304]{2,1,0:T(8,128)(2,1)}), bf16[32,24,2304]{2,1,0:T(8,128)(2,1)}, u32[]{:S(2)}, u32[]{:S(2)}) async-start(bf16[32,24,2304]{2,1,0:T(8,128)(2,1)} %stack.2), calls=%async_computation | async-start | bytes 7077888 | tf_op jit(solution)/shard_map/all_to_all | solution.py:148
  299.6 28.9 %all-to-all-done = bf16[32,24,2304]{2,1,0:T(8,128)(2,1)} async-done(((bf16[32,24,2304]{2,1,0:T(8,128)(2,1)}), bf16[32,24,2304]{2,1,0:T(8,128)(2,1)}, u32[]{:S(2)}, u32[]{:S(2)}) %all-to-all-start) | async-done | bytes 3538976 | tf_op jit(solution)/shard_map/all_to_all | solution.py:148
  328.5 1.5 fusion.74
  330.0 2.0 multiply_reduce_fusion.4
  332.0 1.5 fusion.69
  333.5 2.7 multiply_reduce_fusion.2
  336.3 1.2 multiply_convert_fusion.14
  337.5 2.6 fusion.27
  (72 shorter events, 15.3 us)
Async XLA Ops:
  7.2 2.3 copy-start
  7.2 281.8 %reduce-scatter.4.cloned.1.call-start = ((), (), s32[]{:S(2)}) async-start(), calls=%async_computation.2 | async-start | bytes 3649536
  16.9 3.1 copy-start.14
  16.9 3.2 copy-start.15
  18.1 28.2 %collective-permute-start = (bf16[512,1152]{0,1:T(8,128)(2,1)}, bf16[512,1152]{0,1:T(8,128)(2,1)S(1)}, u32[]{:S(2)}, u32[]{:S(2)}) collective-permute-start(bf16[512,1152]{0,1:T(8,128)(2,1)} %bitcast.1), channel_id=1, source_target_pairs={{0,4},{4,0},{8,12},{12,8},{16,20},{20,16},{24,28},{28,24},{32,36},... | collective-permute-start | bytes 3538952 | tf_op jit(solution)/shard_map/ppermute | solution.py:13
  46.3 1.0 copy-start.5
  48.7 1.3 copy-start.2
  50.0 14.4 %copy-start.3 = (bf16[512,3,6,64]{0,3,2,1:T(8,128)(2,1)S(1)}, bf16[512,3,6,64]{0,3,2,1:T(8,128)(2,1)}, u32[]{:S(2)}) copy-start(bf16[512,3,6,64]{0,3,2,1:T(8,128)(2,1)} %copy-done.2) | copy-start | bytes 3538948
  74.0 10.5 %collective-permute-start.1 = (bf16[512,384]{0,1:T(8,128)(2,1)S(1)}, bf16[512,384]{0,1:T(8,128)(2,1)S(1)}, u32[]{:S(2)}, u32[]{:S(2)}) collective-permute-start(bf16[512,384]{0,1:T(8,128)(2,1)S(1)} %bitcast.60), channel_id=1, source_target_pairs={{0,4},{4,0},{8,12},{12,8},{16,20},{20,16},{24,28},{28,24},{32,36},... | collective-permute-start | bytes 1179656 | tf_op jit(solution)/shard_map/ppermute | solution.py:13
  84.5 1.1 copy-start.7
  84.5 1.5 copy-start.13
  86.0 1.7 copy-start.12
  87.7 5.8 %copy-start.8 = (bf16[512,768]{1,0:T(8,128)(2,1)}, bf16[512,768]{1,0:T(8,128)(2,1)S(1)}, u32[]{:S(2)}) copy-start(bf16[512,768]{1,0:T(8,128)(2,1)S(1)} %fusion.15) | copy-start | bytes 2359300
  89.1 2.0 copy-start.4
  92.9 0.7 copy-start.11
  291.1 2.1 copy-start.9
  293.1 5.9 %copy-start.6 = (bf16[768,768]{1,0:T(8,128)(2,1)S(1)}, bf16[768,768]{1,0:T(8,128)(2,1)}, u32[]{:S(2)}) copy-start(bf16[768,768]{1,0:T(8,128)(2,1)} %param.22) | copy-start | bytes 3538948
  293.1 5.9 %copy-start.10 = (bf16[256,768]{1,0:T(8,128)(2,1)S(1)}, bf16[256,768]{1,0:T(8,128)(2,1)}, u32[]{:S(2)}) copy-start(bf16[256,768]{1,0:T(8,128)(2,1)} %param.21) | copy-start | bytes 1179652
  293.1 35.4 %all-to-all-start = ((bf16[32,24,2304]{2,1,0:T(8,128)(2,1)}), bf16[32,24,2304]{2,1,0:T(8,128)(2,1)}, u32[]{:S(2)}, u32[]{:S(2)}) async-start(bf16[32,24,2304]{2,1,0:T(8,128)(2,1)} %stack.2), calls=%async_computation | async-start | bytes 7077888 | tf_op jit(solution)/shard_map/all_to_all | solution.py:148
  336.3 3.9 %copy-start.1 = (bf16[768,2304]{1,0:T(8,128)(2,1)S(1)}, bf16[768,2304]{1,0:T(8,128)(2,1)}, u32[]{:S(2)}) copy-start(bf16[768,2304]{1,0:T(8,128)(2,1)} %param.15) | copy-start | bytes 10616836
Sparse Core Ops, SparseCore 0:
  111.5 177.4 reduce-scatter.3
